TPU v7x, 32 devices: a whole 2x2x4 slice. The times are simulated.
32 devices in a mesh: tm: 16 (over z, y, x), space: 2 (over core).
Axes of the slice: x: 2, y: 2, z: 4, core: 2. Of those that a mesh axis runs over, the one named last changes fastest.
Arguments:
- traj: float32 [16, 32, 32, 128], P('tm', None, 'space'), may hold values from -6 to 6
- start_state: float32 [32, 32, 128], P(None, 'space'), may hold values from -6 to 6
- actions: float32 [16, 16], P('tm'), may hold values from -6 to 6
- hidden_w: bfloat16 [3, 9, 32, 32], replicated, may hold values from -0.375 to 0.375
- hidden_b: float32 [3, 32], replicated, may hold values from -3 to 3
- head_w: bfloat16 [9, 64, 32], replicated, may hold values from -0.375 to 0.375
- cand_b: float32 [32], replicated, may hold values from -3 to 3
- gate_b: float32 [32], replicated, may hold values from 0 to 9
- skip: float32 [32], replicated, may hold values from 0.1 to 0.9
- act_proj: float32 [16, 64], replicated, may hold values from -1.5 to 1.5
Outputs:
- new_traj: float32 [16, 32, 32, 128], P('tm', None, 'space')
- res_msq: float32 [16], P('tm')
All inputs are finite; a program needn't handle non-finite values.
Results may differ from a plain program's by a relative error of at most 0.0015.
Values may be sent and summed in bfloat16 or wider, within the bound.
A program may use at most 128 MiB of HBM per device.

v0:
```python
import jax
import jax.numpy as jnp
from jax import lax
from jax.sharding import PartitionSpec as P


def extended_2(block, sides, width):
    for axis, dim in sides:
        count = lax.axis_size(axis)
        forward = [(i, i + 1) for i in range(count - 1)]
        backward = [(target, source) for source, target in forward]
        low = lax.ppermute(
            lax.slice_in_dim(block, block.shape[dim] - width, None, axis=dim), axis, forward
        )
        high = lax.ppermute(lax.slice_in_dim(block, 0, width, axis=dim), axis, backward)
        block = jnp.concatenate([low, block, high], axis=dim)
    return block


def from_behind(value, axis, by):
    length = lax.axis_size(axis)
    pairs = [(i, i + by) for i in range(length) if 0 <= i + by < length]
    return lax.ppermute(value, axis, pairs)


def conv_rows(extended, taps):
    rows_out = extended.shape[2] - 2
    width = extended.shape[3]
    padded = jnp.pad(extended, ((0, 0), (0, 0), (0, 0), (1, 1)))
    total = None
    for offa in range(3):
        for offb in range(3):
            term = jnp.einsum(
                "oc,schw->sohw",
                taps[offa * 3 + offb],
                padded[:, :, offa : offa + rows_out, offb : offb + width],
                preferred_element_type=jnp.float32,
            )
            total = term if total is None else total + term
    return total


def rim_rows(hidden):
    return extended_2(hidden, (("space", 2),), 1)


def body(traj, start_state, actions, hidden_w, hidden_b, head_w, cand_b, gate_b, skip, act_proj):
    steps, chans, strip_rows, width = traj.shape
    prior = from_behind(traj[steps - 1].astype(jnp.bfloat16), "tm", 1).astype(jnp.float32)
    first = jnp.where(lax.axis_index("tm") == 0, start_state, prior)
    guess_in = jnp.concatenate([first[None], traj[: steps - 1]], axis=0)
    act_terms = jnp.dot(
        actions, act_proj, precision=lax.Precision.HIGHEST, preferred_element_type=jnp.float32
    )
    hidden = guess_in.astype(jnp.bfloat16)
    layers = hidden_w.shape[0]
    for layer in range(layers):
        pre = conv_rows(rim_rows(hidden), hidden_w[layer]) + hidden_b[layer][None, :, None, None]
        if layer == 0:
            pre = pre + act_terms[:, :chans, None, None]
        hidden = jax.nn.silu(pre).astype(jnp.bfloat16)
    head = conv_rows(rim_rows(hidden), head_w)
    cand = jnp.tanh(
        head[:, :chans] + cand_b[None, :, None, None] + skip[None, :, None, None] * guess_in
    )
    gate = jax.nn.sigmoid(
        head[:, chans:] + gate_b[None, :, None, None] + act_terms[:, chans:, None, None]
    )
    fval = gate * guess_in + (1.0 - gate) * cand
    jac = gate + (1.0 - gate) * (1.0 - cand * cand) * skip[None, :, None, None]
    local_sq = jnp.sum((traj - fval) ** 2, axis=(1, 2, 3))
    total_sq = lax.psum(local_sq, "space")
    res_msq = total_sq / (chans * strip_rows * width * lax.axis_size("space"))
    offs = fval - jac * guess_in

    def compose(carry, pair):
        return ((pair[0] * carry[0], pair[0] * carry[1] + pair[1]), None)

    ones = jnp.ones_like(start_state)
    zeros = jnp.zeros_like(start_state)
    (block_a, block_b), _ = lax.scan(compose, (ones, zeros), (jac, offs))
    blocks = lax.axis_size("tm")
    lines = chans * strip_rows
    share = lines // blocks
    flat_a = block_a.reshape(1, lines, width)
    flat_b = block_b.reshape(1, lines, width)
    maps_a, maps_b = (
        lax.all_to_all(flat_a, "tm", split_axis=1, concat_axis=0, tiled=True),
        lax.all_to_all(flat_b, "tm", split_axis=1, concat_axis=0, tiled=True),
    )
    anchor = lax.dynamic_slice_in_dim(
        start_state.reshape(lines, width), lax.axis_index("tm") * share, share, 0
    )

    def walk(yval, pair):
        return (pair[0] * yval + pair[1], yval)

    _, starts = lax.scan(walk, anchor, (maps_a, maps_b))
    state = lax.all_to_all(starts, "tm", split_axis=0, concat_axis=1, tiled=True).reshape(
        chans, strip_rows, width
    )

    def advance(yval, pair):
        nxt = pair[0] * yval + pair[1]
        return (nxt, nxt)

    _, new_traj = lax.scan(advance, state, (jac, offs))
    return (new_traj, res_msq)


def solution(mesh):
    return jax.shard_map(
        body,
        mesh=mesh,
        in_specs=(
            P("tm", None, "space", None),
            P(None, "space", None),
            P("tm", None),
            P(),
            P(),
            P(),
            P(),
            P(),
            P(),
            P(),
        ),
        out_specs=(P("tm", None, "space", None), P("tm")),
        check_vma=False,
    )
```

profile of v0, /device:TPU:0, one launch (start us, length us, event | category | flops | bytes accessed | tf_op | source)
XLA Modules:
  0.0 97.6 jit_solution(2340202151622617586)
XLA Ops:
  0.7 1.1 %copy.41 = bf16[1,32,16,128]{3,1,2,0:T(8,128)(2,1)S(1)} copy(f32[1,32,16,128]{3,2,1,0:T(8,128)} %param.12) | data formatting | bytes 393216 | tf_op args[0]
  1.7 4.8 %collective-permute-start = (bf16[32,16,128]{2,0,1:T(8,128)(2,1)S(1)}, bf16[32,16,128]{2,0,1:T(8,128)(2,1)S(1)}, u32[]{:S(2)}, u32[]{:S(2)}) collective-permute-start(bf16[32,16,128]{2,0,1:T(8,128)(2,1)S(1)} %bitcast.388), channel_id=1, source_target_pairs={{0,2},{2,4},{4,6},{6,8},{8,10},{10,12},{12,14},{14,16},{16,18},{18... | collective-permute-start | bytes 393224 | tf_op jit(solution)/shard_map/ppermute | solution.py:23
  6.6 0.6 copy-done.9
  7.4 0.6 copy-done.8
  7.9 1.4 %collective-permute-done = bf16[32,16,128]{2,0,1:T(8,128)(2,1)S(1)} collective-permute-done((bf16[32,16,128]{2,0,1:T(8,128)(2,1)S(1)}, bf16[32,16,128]{2,0,1:T(8,128)(2,1)S(1)}, u32[]{:S(2)}, u32[]{:S(2)}) %collective-permute-start) | collective-permute-done | bytes 131104 | tf_op jit(solution)/shard_map/ppermute | solution.py:23
  9.4 1.3 %collective-permute-start.1 = (bf16[1,32,1,128]{3,1,2,0:T(8,128)(2,1)S(1)}, bf16[1,32,1,128]{3,1,2,0:T(8,128)(2,1)S(1)}, u32[]{:S(2)}, u32[]{:S(2)}) collective-permute-start(bf16[1,32,1,128]{3,1,2,0:T(8,128)(2,1)S(1)} %get-tuple-element.88), channel_id=1, source_target_pairs={{0,1},{2,3},{4,5},{6,7},{8,9},{10,11},{12,13},{14,15},{16,17},{18,... | collective-permute-start | bytes 24584 | tf_op jit(solution)/shard_map/ppermute | solution.py:12
  10.7 1.3 %collective-permute-start.2 = (bf16[1,32,1,128]{3,1,2,0:T(8,128)(2,1)S(1)}, bf16[1,32,1,128]{3,1,2,0:T(8,128)(2,1)S(1)}, u32[]{:S(2)}, u32[]{:S(2)}) collective-permute-start(bf16[1,32,1,128]{3,1,2,0:T(8,128)(2,1)S(1)} %get-tuple-element.89), channel_id=1, source_target_pairs={{1,0},{3,2},{5,4},{7,6},{9,8},{11,10},{13,12},{15,14},{17,16},{19,... | collective-permute-start | bytes 24584 | tf_op jit(solution)/shard_map/ppermute | solution.py:15
  12.1 1.7 %collective-permute-done.2 = bf16[1,32,1,128]{3,1,2,0:T(8,128)(2,1)S(1)} collective-permute-done((bf16[1,32,1,128]{3,1,2,0:T(8,128)(2,1)S(1)}, bf16[1,32,1,128]{3,1,2,0:T(8,128)(2,1)S(1)}, u32[]{:S(2)}, u32[]{:S(2)}) %collective-permute-start.2) | collective-permute-done | bytes 8224 | tf_op jit(solution)/shard_map/ppermute | solution.py:15
  15.8 2.1 %collective-permute-start.3 = (bf16[1,32,1,128]{3,1,2,0:T(8,128)(2,1)S(1)}, bf16[1,32,1,128]{3,1,2,0:T(8,128)(2,1)S(1)}, u32[]{:S(2)}, u32[]{:S(2)}) collective-permute-start(bf16[1,32,1,128]{3,1,2,0:T(8,128)(2,1)S(1)} %get-tuple-element.86), channel_id=1, source_target_pairs={{0,1},{2,3},{4,5},{6,7},{8,9},{10,11},{12,13},{14,15},{16,17},{18,... | collective-permute-start | bytes 24584 | tf_op jit(solution)/shard_map/ppermute | solution.py:12
  17.9 1.3 %collective-permute-start.4 = (bf16[1,32,1,128]{3,1,2,0:T(8,128)(2,1)S(1)}, bf16[1,32,1,128]{3,1,2,0:T(8,128)(2,1)S(1)}, u32[]{:S(2)}, u32[]{:S(2)}) collective-permute-start(bf16[1,32,1,128]{3,1,2,0:T(8,128)(2,1)S(1)} %get-tuple-element.87), channel_id=1, source_target_pairs={{1,0},{3,2},{5,4},{7,6},{9,8},{11,10},{13,12},{15,14},{17,16},{19,... | collective-permute-start | bytes 24584 | tf_op jit(solution)/shard_map/ppermute | solution.py:15
  19.2 1.8 %collective-permute-done.4 = bf16[1,32,1,128]{3,1,2,0:T(8,128)(2,1)S(1)} collective-permute-done((bf16[1,32,1,128]{3,1,2,0:T(8,128)(2,1)S(1)}, bf16[1,32,1,128]{3,1,2,0:T(8,128)(2,1)S(1)}, u32[]{:S(2)}, u32[]{:S(2)}) %collective-permute-start.4) | collective-permute-done | bytes 8224 | tf_op jit(solution)/shard_map/ppermute | solution.py:15
  22.9 2.1 %collective-permute-start.5 = (bf16[1,32,1,128]{3,1,2,0:T(8,128)(2,1)S(1)}, bf16[1,32,1,128]{3,1,2,0:T(8,128)(2,1)S(1)}, u32[]{:S(2)}, u32[]{:S(2)}) collective-permute-start(bf16[1,32,1,128]{3,1,2,0:T(8,128)(2,1)S(1)} %get-tuple-element.84), channel_id=1, source_target_pairs={{0,1},{2,3},{4,5},{6,7},{8,9},{10,11},{12,13},{14,15},{16,17},{18,... | collective-permute-start | bytes 24584 | tf_op jit(solution)/shard_map/ppermute | solution.py:12
  25.0 1.3 %collective-permute-start.6 = (bf16[1,32,1,128]{3,1,2,0:T(8,128)(2,1)S(1)}, bf16[1,32,1,128]{3,1,2,0:T(8,128)(2,1)S(1)}, u32[]{:S(2)}, u32[]{:S(2)}) collective-permute-start(bf16[1,32,1,128]{3,1,2,0:T(8,128)(2,1)S(1)} %get-tuple-element.85), channel_id=1, source_target_pairs={{1,0},{3,2},{5,4},{7,6},{9,8},{11,10},{13,12},{15,14},{17,16},{19,... | collective-permute-start | bytes 24584 | tf_op jit(solution)/shard_map/ppermute | solution.py:15
  26.3 1.8 %collective-permute-done.6 = bf16[1,32,1,128]{3,1,2,0:T(8,128)(2,1)S(1)} collective-permute-done((bf16[1,32,1,128]{3,1,2,0:T(8,128)(2,1)S(1)}, bf16[1,32,1,128]{3,1,2,0:T(8,128)(2,1)S(1)}, u32[]{:S(2)}, u32[]{:S(2)}) %collective-permute-start.6) | collective-permute-done | bytes 8224 | tf_op jit(solution)/shard_map/ppermute | solution.py:15
  30.1 2.1 %collective-permute-start.7 = (bf16[1,32,1,128]{3,1,2,0:T(8,128)(2,1)S(1)}, bf16[1,32,1,128]{3,1,2,0:T(8,128)(2,1)S(1)}, u32[]{:S(2)}, u32[]{:S(2)}) collective-permute-start(bf16[1,32,1,128]{3,1,2,0:T(8,128)(2,1)S(1)} %get-tuple-element.82), channel_id=1, source_target_pairs={{0,1},{2,3},{4,5},{6,7},{8,9},{10,11},{12,13},{14,15},{16,17},{18,... | collective-permute-start | bytes 24584 | tf_op jit(solution)/shard_map/ppermute | solution.py:12
  32.2 1.4 %collective-permute-start.8 = (bf16[1,32,1,128]{3,1,2,0:T(8,128)(2,1)S(1)}, bf16[1,32,1,128]{3,1,2,0:T(8,128)(2,1)S(1)}, u32[]{:S(2)}, u32[]{:S(2)}) collective-permute-start(bf16[1,32,1,128]{3,1,2,0:T(8,128)(2,1)S(1)} %get-tuple-element.83), channel_id=1, source_target_pairs={{1,0},{3,2},{5,4},{7,6},{9,8},{11,10},{13,12},{15,14},{17,16},{19,... | collective-permute-start | bytes 24584 | tf_op jit(solution)/shard_map/ppermute | solution.py:15
  33.6 1.8 %collective-permute-done.8 = bf16[1,32,1,128]{3,1,2,0:T(8,128)(2,1)S(1)} collective-permute-done((bf16[1,32,1,128]{3,1,2,0:T(8,128)(2,1)S(1)}, bf16[1,32,1,128]{3,1,2,0:T(8,128)(2,1)S(1)}, u32[]{:S(2)}, u32[]{:S(2)}) %collective-permute-start.8) | collective-permute-done | bytes 8224 | tf_op jit(solution)/shard_map/ppermute | solution.py:15
  35.8 0.3 fusion.43
  36.4 0.3 convolution_add_fusion.5
  37.3 0.3 convolution_add_fusion.2
  38.2 0.6 copy-done.1
  38.9 0.9 multiply_reduce_fusion
  40.0 0.9 copy.25
  41.0 1.0 %bitcast_add_fusion.1 = f32[1,512,128]{2,1,0:T(8,128)S(1)} fusion(f32[1,32,16,128]{3,2,1,0:T(8,128)S(1)} %copy.27, f32[1,32,16,128]{3,2,1,0:T(8,128)} %copy.25), kind=kLoop, calls=%fused_computation.75 | loop fusion | flops 131072 | bytes 786432 | tf_op jit(solution)/shard_map/while/body/eval_jaxpr/add | solution.py:77
  42.0 17.9 %all_to_all.33 = f32[1,512,128]{2,0,1:T(1,128)S(1)} all-to-all(f32[1,512,128]{2,0,1:T(1,128)S(1)} %bitcast.383), channel_id=1, replica_groups=mesh['tm'=16,'space'=2] {'tm'}, dimensions={1} | all-to-all | bytes 524288 | tf_op jit(solution)/shard_map/all_to_all | solution.py:89
  59.9 3.5 %all-to-all-start = ((f32[1,512,128]{2,0,1:T(1,128)}), f32[1,512,128]{2,0,1:T(1,128)S(1)}, u32[]{:S(2)}, u32[]{:S(2)}) async-start(f32[1,512,128]{2,0,1:T(1,128)} %bitcast.132), calls=%async_computation | async-start | bytes 524288 | tf_op jit(solution)/shard_map/all_to_all | solution.py:88
  63.5 9.4 %all-to-all-done = f32[1,512,128]{2,0,1:T(1,128)S(1)} async-done(((f32[1,512,128]{2,0,1:T(1,128)}), f32[1,512,128]{2,0,1:T(1,128)S(1)}, u32[]{:S(2)}, u32[]{:S(2)}) %all-to-all-start) | async-done | bytes 262176 | tf_op jit(solution)/shard_map/all_to_all | solution.py:88
  72.9 9.9 %while.2 = (s32[]{:T(128)}, f32[32,128]{1,0:T(8,128)S(1)}, f32[16,32,128]{2,1,0:T(8,128)}, f32[16,32,128]{2,1,0:T(8,128)S(1)}, f32[16,32,128]{2,1,0:T(8,128)S(1)}, /*index=5*/s32[]{:T(128)}) while((s32[]{:T(128)}, f32[32,128]{1,0:T(8,128)S(1)}, f32[16,32,128]{2,1,0:T(8,128)}, f32[16,32,128]{2,1,0:T(8,128)S(1)}, f32[16,32,128]{2,1,0:T(8,128)S(1)}, ...), condition=%wide.region_1.2_spmd, body=%wide.region_0.1_spmd.sunk | while | flops 8194 | bytes 98889 | solution.py:98
  72.9 0.6 bitcast_dynamic-update-slice_fusion.2
  73.5 0.6 bitcast_dynamic-update-slice_fusion.2
  74.1 0.6 bitcast_dynamic-update-slice_fusion.2
  74.7 0.6 bitcast_dynamic-update-slice_fusion.2
  75.4 0.6 bitcast_dynamic-update-slice_fusion.2
  76.0 0.6 bitcast_dynamic-update-slice_fusion.2
  76.6 0.6 bitcast_dynamic-update-slice_fusion.2
  77.2 0.6 bitcast_dynamic-update-slice_fusion.2
  77.8 0.6 bitcast_dynamic-update-slice_fusion.2
  78.4 0.6 bitcast_dynamic-update-slice_fusion.2
  79.1 0.6 bitcast_dynamic-update-slice_fusion.2
  79.7 0.6 bitcast_dynamic-update-slice_fusion.2
  80.3 0.6 bitcast_dynamic-update-slice_fusion.2
  80.9 0.6 bitcast_dynamic-update-slice_fusion.2
  81.5 0.6 bitcast_dynamic-update-slice_fusion.2
  82.1 0.6 bitcast_dynamic-update-slice_fusion.2
  82.7 3.5 %all-to-all-start.2 = ((f32[16,32,128]{2,1,0:T(8,128)}), f32[16,32,128]{2,1,0:T(8,128)S(1)}, u32[]{:S(2)}, u32[]{:S(2)}) async-start(f32[16,32,128]{2,1,0:T(8,128)} %get-tuple-element.54), calls=%async_computation.2 | async-start | bytes 524288 | tf_op jit(solution)/shard_map/all_to_all | solution.py:99
  86.3 3.0 %psum.7 = f32[1]{0:T(128)} all-reduce(f32[1]{0:T(128)} %bitcast.139), channel_id=1, replica_groups=mesh['tm'=16,'space'=2] {'space'}, use_global_device_ids=true, to_apply=%region_3.4 | all-reduce | flops 1 | bytes 8 | tf_op jit(solution)/shard_map/psum | solution.py:72
  89.9 5.6 %all-to-all-done.2 = f32[16,32,128]{2,1,0:T(8,128)S(1)} async-done(((f32[16,32,128]{2,1,0:T(8,128)}), f32[16,32,128]{2,1,0:T(8,128)S(1)}, u32[]{:S(2)}, u32[]{:S(2)}) %all-to-all-start.2) | async-done | bytes 262176 | tf_op jit(solution)/shard_map/all_to_all | solution.py:99
  95.6 0.9 copy.31
  (87 shorter events, 8.5 us)
Async XLA Ops:
  0.6 6.0 %copy-start = (f32[16,64]{1,0:T(8,128)S(1)}, f32[16,64]{1,0:T(8,128)}, u32[]{:S(2)}) copy-start(f32[16,64]{1,0:T(8,128)} %param.21) | copy-start | bytes 12292
  0.6 8.7 %copy-start.2 = (f32[32,16,128]{2,1,0:T(8,128)S(1)}, f32[32,16,128]{2,1,0:T(8,128)}, u32[]{:S(2)}) copy-start(f32[32,16,128]{2,1,0:T(8,128)} %param.13) | copy-start | bytes 786436
  1.7 7.6 %collective-permute-start = (bf16[32,16,128]{2,0,1:T(8,128)(2,1)S(1)}, bf16[32,16,128]{2,0,1:T(8,128)(2,1)S(1)}, u32[]{:S(2)}, u32[]{:S(2)}) collective-permute-start(bf16[32,16,128]{2,0,1:T(8,128)(2,1)S(1)} %bitcast.388), channel_id=1, source_target_pairs={{0,2},{2,4},{4,6},{6,8},{8,10},{10,12},{12,14},{14,16},{16,18},{18... | collective-permute-start | bytes 393224 | tf_op jit(solution)/shard_map/ppermute | solution.py:23
  6.6 0.7 copy-start.9
  7.3 0.7 copy-start.8
  9.4 2.7 %collective-permute-start.1 = (bf16[1,32,1,128]{3,1,2,0:T(8,128)(2,1)S(1)}, bf16[1,32,1,128]{3,1,2,0:T(8,128)(2,1)S(1)}, u32[]{:S(2)}, u32[]{:S(2)}) collective-permute-start(bf16[1,32,1,128]{3,1,2,0:T(8,128)(2,1)S(1)} %get-tuple-element.88), channel_id=1, source_target_pairs={{0,1},{2,3},{4,5},{6,7},{8,9},{10,11},{12,13},{14,15},{16,17},{18,... | collective-permute-start | bytes 24584 | tf_op jit(solution)/shard_map/ppermute | solution.py:12
  10.7 3.1 %collective-permute-start.2 = (bf16[1,32,1,128]{3,1,2,0:T(8,128)(2,1)S(1)}, bf16[1,32,1,128]{3,1,2,0:T(8,128)(2,1)S(1)}, u32[]{:S(2)}, u32[]{:S(2)}) collective-permute-start(bf16[1,32,1,128]{3,1,2,0:T(8,128)(2,1)S(1)} %get-tuple-element.89), channel_id=1, source_target_pairs={{1,0},{3,2},{5,4},{7,6},{9,8},{11,10},{13,12},{15,14},{17,16},{19,... | collective-permute-start | bytes 24584 | tf_op jit(solution)/shard_map/ppermute | solution.py:15
  12.1 1.9 %copy-start.3 = (bf16[3,9,32,32]{3,2,1,0:T(8,128)(2,1)S(1)}, bf16[3,9,32,32]{3,2,1,0:T(8,128)(2,1)}, u32[]{:S(2)}) copy-start(bf16[3,9,32,32]{3,2,1,0:T(8,128)(2,1)} %param.15) | copy-start | bytes 165892
  15.8 3.4 %collective-permute-start.3 = (bf16[1,32,1,128]{3,1,2,0:T(8,128)(2,1)S(1)}, bf16[1,32,1,128]{3,1,2,0:T(8,128)(2,1)S(1)}, u32[]{:S(2)}, u32[]{:S(2)}) collective-permute-start(bf16[1,32,1,128]{3,1,2,0:T(8,128)(2,1)S(1)} %get-tuple-element.86), channel_id=1, source_target_pairs={{0,1},{2,3},{4,5},{6,7},{8,9},{10,11},{12,13},{14,15},{16,17},{18,... | collective-permute-start | bytes 24584 | tf_op jit(solution)/shard_map/ppermute | solution.py:12
  17.9 3.1 %collective-permute-start.4 = (bf16[1,32,1,128]{3,1,2,0:T(8,128)(2,1)S(1)}, bf16[1,32,1,128]{3,1,2,0:T(8,128)(2,1)S(1)}, u32[]{:S(2)}, u32[]{:S(2)}) collective-permute-start(bf16[1,32,1,128]{3,1,2,0:T(8,128)(2,1)S(1)} %get-tuple-element.87), channel_id=1, source_target_pairs={{1,0},{3,2},{5,4},{7,6},{9,8},{11,10},{13,12},{15,14},{17,16},{19,... | collective-permute-start | bytes 24584 | tf_op jit(solution)/shard_map/ppermute | solution.py:15
  22.9 3.4 %collective-permute-start.5 = (bf16[1,32,1,128]{3,1,2,0:T(8,128)(2,1)S(1)}, bf16[1,32,1,128]{3,1,2,0:T(8,128)(2,1)S(1)}, u32[]{:S(2)}, u32[]{:S(2)}) collective-permute-start(bf16[1,32,1,128]{3,1,2,0:T(8,128)(2,1)S(1)} %get-tuple-element.84), channel_id=1, source_target_pairs={{0,1},{2,3},{4,5},{6,7},{8,9},{10,11},{12,13},{14,15},{16,17},{18,... | collective-permute-start | bytes 24584 | tf_op jit(solution)/shard_map/ppermute | solution.py:12
  25.0 3.1 %collective-permute-start.6 = (bf16[1,32,1,128]{3,1,2,0:T(8,128)(2,1)S(1)}, bf16[1,32,1,128]{3,1,2,0:T(8,128)(2,1)S(1)}, u32[]{:S(2)}, u32[]{:S(2)}) collective-permute-start(bf16[1,32,1,128]{3,1,2,0:T(8,128)(2,1)S(1)} %get-tuple-element.85), channel_id=1, source_target_pairs={{1,0},{3,2},{5,4},{7,6},{9,8},{11,10},{13,12},{15,14},{17,16},{19,... | collective-permute-start | bytes 24584 | tf_op jit(solution)/shard_map/ppermute | solution.py:15
  30.1 3.5 %collective-permute-start.7 = (bf16[1,32,1,128]{3,1,2,0:T(8,128)(2,1)S(1)}, bf16[1,32,1,128]{3,1,2,0:T(8,128)(2,1)S(1)}, u32[]{:S(2)}, u32[]{:S(2)}) collective-permute-start(bf16[1,32,1,128]{3,1,2,0:T(8,128)(2,1)S(1)} %get-tuple-element.82), channel_id=1, source_target_pairs={{0,1},{2,3},{4,5},{6,7},{8,9},{10,11},{12,13},{14,15},{16,17},{18,... | collective-permute-start | bytes 24584 | tf_op jit(solution)/shard_map/ppermute | solution.py:12
  32.1 3.4 %copy-start.4 = (bf16[9,64,32]{1,2,0:T(8,128)(2,1)S(1)}, bf16[9,64,32]{1,2,0:T(8,128)(2,1)}, u32[]{:S(2)}) copy-start(bf16[9,64,32]{1,2,0:T(8,128)(2,1)} %param.17) | copy-start | bytes 110596
  32.2 3.2 %collective-permute-start.8 = (bf16[1,32,1,128]{3,1,2,0:T(8,128)(2,1)S(1)}, bf16[1,32,1,128]{3,1,2,0:T(8,128)(2,1)S(1)}, u32[]{:S(2)}, u32[]{:S(2)}) collective-permute-start(bf16[1,32,1,128]{3,1,2,0:T(8,128)(2,1)S(1)} %get-tuple-element.83), channel_id=1, source_target_pairs={{1,0},{3,2},{5,4},{7,6},{9,8},{11,10},{13,12},{15,14},{17,16},{19,... | collective-permute-start | bytes 24584 | tf_op jit(solution)/shard_map/ppermute | solution.py:15
  37.9 1.0 copy-start.1
  38.1 0.7 copy-start.5
  38.2 0.7 copy-start.6
  38.2 0.7 copy-start.7
  59.9 13.0 %all-to-all-start = ((f32[1,512,128]{2,0,1:T(1,128)}), f32[1,512,128]{2,0,1:T(1,128)S(1)}, u32[]{:S(2)}, u32[]{:S(2)}) async-start(f32[1,512,128]{2,0,1:T(1,128)} %bitcast.132), calls=%async_computation | async-start | bytes 524288 | tf_op jit(solution)/shard_map/all_to_all | solution.py:88
  82.7 12.8 %all-to-all-start.2 = ((f32[16,32,128]{2,1,0:T(8,128)}), f32[16,32,128]{2,1,0:T(8,128)S(1)}, u32[]{:S(2)}, u32[]{:S(2)}) async-start(f32[16,32,128]{2,1,0:T(8,128)} %get-tuple-element.54), calls=%async_computation.2 | async-start | bytes 524288 | tf_op jit(solution)/shard_map/all_to_all | solution.py:99
where the time goes:
time: 98.3 us; the launch traced here: 97.6 us
  starting transfers between devices  24.8 us (25%)
  waiting for transfers between devices  23.3 us (24%)
  blocking collectives  20.8 us (21%)
  local copies, waits for them, and re-layouts  14.7 us (15%)
  matrix products  7.88 us (8%)
  other arithmetic  3.1 us (3%)
  between operations  2.97 us (3%)
    all_to_all x1, blocking collectives, body(): lax.all_to_all(flat_b, 'tm', split_axis=1, concat_axis=0, tiled=True)  17.9 us
    dynamic_update_slice x16, local copies, waits for them, and re-layouts, body(): _, starts = lax.scan(walk, anchor, (maps_a, maps_b))  9.74 us
    all_to_all x1, waiting for transfers between devices, body(): lax.all_to_all(flat_a, 'tm', split_axis=1, concat_axis=0, tiled=True)  9.43 us
    dot_general x36, matrix products, conv_rows(): jnp.einsum('oc,schw->sohw', taps[offa * 3 + offb], padded[:, :, offa:offa...  7.76 us
    ppermute x4, starting transfers between devices, extended_2(): lax.ppermute(lax.slice_in_dim(block, block.shape[dim] - width, None, axis...  7.52 us
    ppermute x4, waiting for transfers between devices, extended_2(): lax.ppermute(lax.slice_in_dim(block, 0, width, axis=dim), axis, backward)  6.96 us
    all_to_all x1, waiting for transfers between devices, body(): lax.all_to_all(starts, 'tm', split_axis=0, concat_axis=1, tiled=True)  5.57 us
    ppermute x4, starting transfers between devices, extended_2(): lax.ppermute(lax.slice_in_dim(block, 0, width, axis=dim), axis, backward)  5.3 us
  transfers between devices with their start and end apart: 11, of which 7 were waited for; matrix products, arithmetic and copies ran while one was open for 0% of the time, Pallas kernels for 0%

commit v1 on v0

v1 whole, which is shorter than its diff:
```python
import functools

import jax
import jax.numpy as jnp
from jax import lax
from jax.experimental import pallas as pl
from jax.experimental.pallas import tpu as pltpu
from jax.sharding import PartitionSpec as P

MESH = pl.DeviceIdType.MESH
Q = 2
PARTS = 4
VMEM = pltpu.VMEM


def column(row):
    n = row.shape[1]
    eye = lax.broadcasted_iota(jnp.int32, (n, n), 0) == lax.broadcasted_iota(jnp.int32, (n, n), 1)
    return jnp.sum(jnp.where(eye, jnp.broadcast_to(row, (n, n)), 0.0), axis=1, keepdims=True)


def kernel(
    T, S, G, K, C, R, W, layers,
    traj_h, start_h, actions, hw, hb, headw, cand_b, gate_b, skip_r, proj,
    out, res,
    traj, start, sendb, ext, ha, hbuf, wh, wo, start_r, guess, ab, rab, cin, cout, ys, st, part, rpart,
    s_in, s_prior, r_prior, s_ab, r_ab, s_ch, r_ch, s_st, r_st, s_ps, r_ps,
):
    H = layers + 1
    L = R * C // G
    CH = L // K
    NG = T // G
    RG = R // G
    t = lax.axis_index("tm")
    s = lax.axis_index("space")
    g = t // G
    m = lax.rem(t, G)
    base = g * G
    nxt, prv = lax.rem(t + 1, T), lax.rem(t + T - 1, T)
    peers = []
    for tt in (nxt, prv):
        for ds in sorted({0, 1 % S, (S - 1) % S}):
            peers.append((tt, lax.rem(s + ds, S)))
    for p in range(1, G):
        peers.append((base + lax.rem(m + p, G), s))
    for step in (G, T - G):
        if NG > 1:
            peers.append((lax.rem(t + step, T), s))
    for p in range(1, S):
        peers.append((t, lax.rem(s + p, S)))
    load_t = pltpu.make_async_copy(traj_h, traj, s_in.at[0])
    load_s = pltpu.make_async_copy(start_h, start, s_in.at[1])
    load_t.start()
    load_s.start()
    barrier = pltpu.get_barrier_semaphore()
    for peer in peers:
        pl.semaphore_signal(barrier, inc=1, device_id=peer, device_id_type=MESH)

    last = t == T - 1
    load_t.wait()
    load_s.wait()
    for r in range(R):
        begin = start[pl.ds(r, C, stride=R), :]
        start_r[pl.ds(r * C, C), :] = begin
        sendb[pl.ds(r * C, C), :] = jnp.where(last, begin, traj[pl.ds(r, C, stride=R), :]).astype(jnp.bfloat16)

    pl.semaphore_wait(barrier, len(peers))

    def prior_copy(i, src, dst, to):
        return pltpu.make_async_remote_copy(
            src_ref=src, dst_ref=dst, send_sem=s_prior.at[i], recv_sem=r_prior.at[i],
            device_id=(nxt, to), device_id_type=MESH)

    up, down = s > 0, s < S - 1
    to_down = prior_copy(0, sendb.at[pl.ds((R - H) * C, H * C)], ext.at[pl.ds(0, H * C)], lax.rem(s + 1, S))
    to_up = prior_copy(1, sendb.at[pl.ds(0, H * C)], ext.at[pl.ds((R + H) * C, H * C)], lax.rem(s + S - 1, S))
    PR = R // PARTS
    main = [
        prior_copy(2 + i, sendb.at[pl.ds(i * PR * C, PR * C)], ext.at[pl.ds((H + i * PR) * C, PR * C)], s)
        for i in range(PARTS)
    ]

    @pl.when(down)
    def _():
        to_down.start()

    for copy in main:
        copy.start()

    @pl.when(up)
    def _():
        to_up.start()

    wh[...] = jnp.zeros_like(wh)
    wo[...] = jnp.zeros_like(wo)
    taps = [headw[pl.ds(k * C, C), :].astype(jnp.float32).T.astype(jnp.bfloat16) for k in range(9)]
    for q in range(Q):
        for a in range(3):
            for b in range(3):
                at = ((q + a) * 3 + b) * C
                for l in range(layers):
                    wh[l, pl.ds(q * C, C), pl.ds(at, C)] = hw[pl.ds((l * 9 + 3 * a + b) * C, C), :]
                wo[pl.ds(q * 2 * C, 2 * C), pl.ds(at, C)] = taps[3 * a + b]
    act = column(jnp.sum(column(actions[...]) * proj[...], axis=0, keepdims=True))
    biases = [column(hb[pl.ds(l, 1), :]) for l in range(layers)]
    biases[0] = biases[0] + act[:C]
    cb = column(cand_b[...])
    gb = column(gate_b[...]) + act[C:]
    skip = column(skip_r[...])
    lane = lax.broadcasted_iota(jnp.int32, (C, W), 1)

    def put(buf, row, x):
        buf[pl.ds(row * 3 * C, C), :] = jnp.where(lane == 0, 0.0, pltpu.roll(x, 1, 1)).astype(jnp.bfloat16)
        buf[pl.ds(row * 3 * C + C, C), :] = x.astype(jnp.bfloat16)
        buf[pl.ds(row * 3 * C + 2 * C, C), :] = jnp.where(lane == W - 1, 0.0, pltpu.roll(x, W - 1, 1)).astype(jnp.bfloat16)

    upf, downf = up.astype(jnp.float32), down.astype(jnp.float32)

    def arrive(r):
        if r == 0:
            @pl.when(up)
            def _():
                to_down.wait_recv()

            @pl.when(jnp.logical_not(up))
            def _():
                ext[pl.ds(0, H * C), :] = jnp.zeros((H * C, W), jnp.bfloat16)
        elif r == R + H:
            @pl.when(down)
            def _():
                to_up.wait_recv()

            @pl.when(jnp.logical_not(down))
            def _():
                ext[pl.ds((R + H) * C, H * C), :] = jnp.zeros((H * C, W), jnp.bfloat16)
        elif H <= r < R + H and (r - H) % PR == 0:
            main[(r - H) // PR].wait_recv()
        x = ext[pl.ds(r * C, C), :].astype(jnp.float32)
        put(ha, r, x)
        if H <= r < R + H:
            guess[pl.ds((r - H) * C, C), :] = jnp.where(t == 0, start_r[pl.ds((r - H) * C, C), :], x)

    src, dst = ha, hbuf
    wide = (Q + 2) * 3 * C

    def gather(buf, first, count):
        parts = []
        for i in range(count):
            at = (first + Q * i) * 3 * C
            parts.append(buf[pl.ds(at if isinstance(at, int) else pl.multiple_of(at, 3 * C), wide), :])
        return jnp.concatenate(parts, axis=1)

    here = 0
    for l in range(layers):
        rows = R + 2 * (H - 1 - l)
        edge = H - 1 - l
        pairs = rows // Q
        for lo in range(0, pairs, 2):
            count = min(2, pairs - lo)
            if l == 0:
                while here < Q * (lo + count) + 2:
                    arrive(here)
                    here += 1
            o = jnp.dot(wh[l], gather(src, Q * lo, count), preferred_element_type=jnp.float32)
            for i in range(count):
                for q in range(Q):
                    row = Q * (lo + i) + q
                    pre = o[q * C:(q + 1) * C, i * W:(i + 1) * W] + biases[l]
                    h = pre * jax.nn.sigmoid(pre)
                    if row < edge:
                        h = h * upf
                    elif row >= R + edge:
                        h = h * downf
                    put(dst, row, h)
        src, dst = dst, src

    def ab_copy(p, j):
        return pltpu.make_async_remote_copy(
            src_ref=ab.at[j], dst_ref=rab.at[m], send_sem=s_ab.at[p], recv_sem=r_ab.at[p],
            device_id=(base + j, s), device_id_type=MESH)

    acc = jnp.zeros((C, W), jnp.float32)
    for p in range(1, G + 1):
        j = lax.rem(m + p, G)
        for lo in range(0, RG // Q, 2):
            count = min(2, RG // Q - lo)
            o = jnp.dot(wo[...], gather(src, j * RG + Q * lo, count), preferred_element_type=jnp.float32)
            for i in range(count):
                for q in range(Q):
                    own = Q * (lo + i) + q
                    row = j * RG + own
                    hd = o[q * 2 * C:(q + 1) * 2 * C, i * W:(i + 1) * W]
                    x = guess[pl.ds(pl.multiple_of(row * C, C), C), :]
                    cand = jnp.tanh(hd[:C] + cb + skip * x)
                    gate = jax.nn.sigmoid(hd[C:] + gb)
                    f = gate * x + (1.0 - gate) * cand
                    jac = gate + (1.0 - gate) * (1.0 - cand * cand) * skip
                    d = traj[pl.ds(row, C, stride=R), :] - f
                    acc = acc + d * d
                    ab[j, 0, pl.ds(own * C, C), :] = jac
                    ab[j, 1, pl.ds(own * C, C), :] = f - jac * x
        if p < G:
            ab_copy(p, j).start()
    rab[m] = ab[m]
    part[...] = jnp.sum(acc.reshape(C // 8, 8, W), axis=0)

    def ps_copy(p):
        return pltpu.make_async_remote_copy(
            src_ref=part, dst_ref=rpart.at[p - 1], send_sem=s_ps.at[p - 1], recv_sem=r_ps.at[p - 1],
            device_id=(t, lax.rem(s + p, S)), device_id_type=MESH)

    for p in range(1, S):
        ps_copy(p).start()
    for p in range(1, G):
        ab_copy(p, lax.rem(m + p, G)).wait_recv()

    def chain(k):
        return pltpu.make_async_remote_copy(
            src_ref=cout.at[k], dst_ref=cin.at[k], send_sem=s_ch.at[k], recv_sem=r_ch.at[k],
            device_id=(lax.rem(t + G, T), s), device_id_type=MESH)

    def st_copy(p, k):
        j = lax.rem(m + p, G)
        return pltpu.make_async_remote_copy(
            src_ref=ys.at[j, k], dst_ref=st.at[m, k], send_sem=s_st.at[p, k], recv_sem=r_st.at[p, k],
            device_id=(base + j, s), device_id_type=MESH)

    for k in range(K):
        @pl.when(g == 0)
        def _():
            cin[k] = start_r[pl.ds(m * L + k * CH, CH), :]

        @pl.when(g > 0)
        def _():
            chain(k).wait_recv()

        y = cin[k]
        for j in range(G):
            ys[j, k] = y
            y = rab[j, 0, pl.ds(k * CH, CH), :] * y + rab[j, 1, pl.ds(k * CH, CH), :]
        cout[k] = y

        @pl.when(g < NG - 1)
        def _():
            chain(k).start()

        @pl.when(g == NG - 1)
        def _():
            for p in range(1, G):
                st_copy(p, k).start()

    @pl.when(g < NG - 1)
    def _():
        for k in range(K):
            for p in range(1, G):
                st_copy(p, k).start()

    total = part[...]
    for p in range(1, S):
        ps_copy(p).wait_recv()
        total = total + rpart[p - 1]
    res[0] = jnp.sum(total) * (1.0 / (C * R * S * W))

    for k in range(K):
        for p in range(G):
            j = lax.rem(m + G - p, G)
            if p > 0:
                st_copy(p, k).wait_recv()
                y = st[j, k]
            else:
                y = ys[m, k]
            for i in range(CH // C):
                own = k * (CH // C) + i
                out[pl.ds(j * RG + own, C, stride=R), :] = (
                    ab[j, 0, pl.ds(own * C, C), :] * y[i * C:(i + 1) * C] + ab[j, 1, pl.ds(own * C, C), :])

    for copy in main:
        copy.wait_send()

    @pl.when(down)
    def _():
        to_down.wait_send()

    @pl.when(up)
    def _():
        to_up.wait_send()

    for p in range(1, S):
        ps_copy(p).wait_send()
    for p in range(1, G):
        ab_copy(p, lax.rem(m + p, G)).wait_send()
        for k in range(K):
            st_copy(p, k).wait_send()

    @pl.when(g < NG - 1)
    def _():
        for k in range(K):
            chain(k).wait_send()


def group_of(T, R):
    best = 1
    for n in range(1, T + 1):
        if T % n == 0 and R % n == 0 and n * n <= T:
            best = n
    return best


def body(T, S, traj, start, actions, hw, hb, headw, cand_b, gate_b, skip, proj):
    steps, C, R, W = traj.shape
    layers = hw.shape[0]
    G = group_of(T, R)
    K = R // G
    H = layers + 1
    L = R * C // G
    CH = L // K
    f32, bf16 = jnp.float32, jnp.bfloat16
    wide = (Q + 2) * 3 * C
    DMA = pltpu.SemaphoreType.DMA
    spec = pl.BlockSpec(memory_space=VMEM)
    new, res = pl.pallas_call(
        functools.partial(kernel, T, S, G, K, C, R, W, layers),
        out_shape=(jax.ShapeDtypeStruct((C * R, W), f32), jax.ShapeDtypeStruct((1,), f32)),
        in_specs=[pl.BlockSpec(memory_space=pltpu.HBM)] * 2 + [spec] * 8,
        out_specs=(spec, pl.BlockSpec(memory_space=pltpu.SMEM)),
        scratch_shapes=[
            VMEM((C * R, W), f32),
            VMEM((C * R, W), f32),
            VMEM((R * C, W), bf16),
            VMEM(((R + 2 * H) * C, W), bf16),
            VMEM(((R + 2 * H) * 3 * C, W), bf16),
            VMEM(((R + 2 * H) * 3 * C, W), bf16),
            VMEM((layers, Q * C, wide), bf16),
            VMEM((Q * 2 * C, wide), bf16),
            VMEM((R * C, W), f32),
            VMEM((R * C, W), f32),
            VMEM((G, 2, L, W), f32),
            VMEM((G, 2, L, W), f32),
            VMEM((K, CH, W), f32),
            VMEM((K, CH, W), f32),
            VMEM((G, K, CH, W), f32),
            VMEM((G, K, CH, W), f32),
            VMEM((8, W), f32),
            VMEM((max(S - 1, 1), 8, W), f32),
            DMA((2,)),
            DMA((2 + PARTS,)), DMA((2 + PARTS,)),
            DMA((G,)), DMA((G,)),
            DMA((K,)), DMA((K,)),
            DMA((G, K)), DMA((G, K)),
            DMA((max(S - 1, 1),)), DMA((max(S - 1, 1),)),
        ],
        compiler_params=pltpu.CompilerParams(
            collective_id=0, has_side_effects=True, vmem_limit_bytes=63 * 1024 * 1024),
    )(
        traj.reshape(C * R, W), start.reshape(C * R, W), actions,
        hw.reshape(-1, hw.shape[-1]), hb, headw.swapaxes(1, 2).reshape(-1, headw.shape[1]),
        cand_b.reshape(1, C), gate_b.reshape(1, C), skip.reshape(1, C), proj,
    )
    return new.reshape(traj.shape), res


def solution(mesh):
    return jax.shard_map(
        functools.partial(body, mesh.shape["tm"], mesh.shape["space"]),
        mesh=mesh,
        in_specs=(
            P("tm", None, "space", None),
            P(None, "space", None),
            P("tm", None),
            P(), P(), P(), P(), P(), P(), P(),
        ),
        out_specs=(P("tm", None, "space", None), P("tm")),
        check_vma=False,
    )
```

time: 98.3 us -> 36.6 us (0.37)
  the two profiles are of different devices: /device:TPU:0 before, /device:TPU:24 now
where the time goes in v1:
time: 36.6 us; the launch traced here: 36.4 us
  Pallas kernels  32.3 us (88%)
  between operations  2.41 us (7%)
  local copies, waits for them, and re-layouts  1.67 us (5%)
    pallas_call x1, Pallas kernels, body(): pl.pallas_call(functools.partial(kernel, T, S, G, K, C, R, W, layers), ou...  32.3 us
    unnamed x1, local copies, waits for them, and re-layouts  1.67 us

profile of v1, /device:TPU:24, one launch (start us, length us, event | category | flops | bytes accessed | tf_op | source)
XLA Modules:
  0.0 36.4 jit_solution(10720052646086622322)
XLA Ops:
  0.6 32.3 %shard_map.113 = (f32[512,128]{1,0:T(8,128)}, f32[1]{0:T(128)}) custom-call(f32[512,128]{1,0:T(8,128)} %bitcast.10, f32[512,128]{1,0:T(8,128)} %bitcast.11, f32[1,16]{1,0:T(1,128)} %actions.1, bf16[864,32]{1,0:T(8,128)(2,1)} %bitcast.13, f32[3,32]{1,0:T(4,128)} %hb.1, bf16[288,64]{1,0:T(8,128)(2,1)} %bitcast.14, f32[1,32]{1,0:T(1,128)} %bitcast.15, ...), custom_call_target="tpu_custom_call" | custom-call | tf_op jit(solution)/shard_map/pallas_call | solution.py:321
  32.9 1.7 %copy.14 = f32[1,32,16,128]{3,2,1,0:T(8,128)} copy(f32[1,32,16,128]{3,2,1,0:T(8,128)} %bitcast.12) | data formatting | bytes 524288

commit v2 on v1

--- a/solution.py
+++ b/solution.py
@@ -9,7 +9,6 @@
 
 MESH = pl.DeviceIdType.MESH
 Q = 2
-PARTS = 4
 VMEM = pltpu.VMEM
 
 
@@ -23,12 +22,13 @@
     T, S, G, K, C, R, W, layers,
     traj_h, start_h, actions, hw, hb, headw, cand_b, gate_b, skip_r, proj,
     out, res,
-    traj, start, sendb, ext, ha, hbuf, wh, wo, start_r, guess, ab, rab, cin, cout, ys, st, part, rpart,
-    s_in, s_prior, r_prior, s_ab, r_ab, s_ch, r_ch, s_st, r_st, s_ps, r_ps,
+    traj, start, sendb, ext, tnext, actn, f0, ha, hbuf, wh, wo, guess, ab, rab, cin, cout, ys, st, part, rpart,
+    s_in, s_prior, r_prior, s_ab, r_ab, s_ch, r_ch, s_st, r_st, s_ps, r_ps, s_f0, r_f0,
 ):
     H = layers + 1
     L = R * C // G
     CH = L // K
+    per = CH // C
     NG = T // G
     RG = R // G
     t = lax.axis_index("tm")
@@ -39,7 +39,7 @@
     nxt, prv = lax.rem(t + 1, T), lax.rem(t + T - 1, T)
     peers = []
     for tt in (nxt, prv):
-        for ds in sorted({0, 1 % S, (S - 1) % S}):
+        for ds in range(S):
             peers.append((tt, lax.rem(s + ds, S)))
     for p in range(1, G):
         peers.append((base + lax.rem(m + p, G), s))
@@ -53,43 +53,20 @@
     load_t.start()
     load_s.start()
     barrier = pltpu.get_barrier_semaphore()
+    last = t == T - 1
+    early = t < G
     for peer in peers:
         pl.semaphore_signal(barrier, inc=1, device_id=peer, device_id_type=MESH)
 
-    last = t == T - 1
-    load_t.wait()
-    load_s.wait()
-    for r in range(R):
-        begin = start[pl.ds(r, C, stride=R), :]
-        start_r[pl.ds(r * C, C), :] = begin
-        sendb[pl.ds(r * C, C), :] = jnp.where(last, begin, traj[pl.ds(r, C, stride=R), :]).astype(jnp.bfloat16)
-
-    pl.semaphore_wait(barrier, len(peers))
-
-    def prior_copy(i, src, dst, to):
-        return pltpu.make_async_remote_copy(
-            src_ref=src, dst_ref=dst, send_sem=s_prior.at[i], recv_sem=r_prior.at[i],
-            device_id=(nxt, to), device_id_type=MESH)
-
-    up, down = s > 0, s < S - 1
-    to_down = prior_copy(0, sendb.at[pl.ds((R - H) * C, H * C)], ext.at[pl.ds(0, H * C)], lax.rem(s + 1, S))
-    to_up = prior_copy(1, sendb.at[pl.ds(0, H * C)], ext.at[pl.ds((R + H) * C, H * C)], lax.rem(s + S - 1, S))
-    PR = R // PARTS
-    main = [
-        prior_copy(2 + i, sendb.at[pl.ds(i * PR * C, PR * C)], ext.at[pl.ds((H + i * PR) * C, PR * C)], s)
-        for i in range(PARTS)
-    ]
-
-    @pl.when(down)
-    def _():
-        to_down.start()
-
-    for copy in main:
-        copy.start()
-
-    @pl.when(up)
-    def _():
-        to_up.start()
+
+    @pl.when(early)
+    def _():
+        pl.semaphore_signal(barrier, inc=1, device_id=(T - 1, s), device_id_type=MESH)
+
+    @pl.when(last)
+    def _():
+        for j in range(G):
+            pl.semaphore_signal(barrier, inc=1, device_id=(j, s), device_id_type=MESH)
 
     wh[...] = jnp.zeros_like(wh)
     wo[...] = jnp.zeros_like(wo)
@@ -101,7 +78,40 @@
                 for l in range(layers):
                     wh[l, pl.ds(q * C, C), pl.ds(at, C)] = hw[pl.ds((l * 9 + 3 * a + b) * C, C), :]
                 wo[pl.ds(q * 2 * C, 2 * C), pl.ds(at, C)] = taps[3 * a + b]
-    act = column(jnp.sum(column(actions[...]) * proj[...], axis=0, keepdims=True))
+    load_t.wait()
+    load_s.wait()
+    for r in range(R):
+        row = traj[pl.ds(r, C, stride=R), :]
+        x = jnp.where(last, start[pl.ds(r, C, stride=R), :], row)
+        guess[pl.ds(r * C, C), :] = x
+        ext[pl.ds((H + r) * C, C), :] = x.astype(jnp.bfloat16)
+        sendb[pl.ds(r * C, C), :] = row.astype(jnp.bfloat16)
+
+    pl.semaphore_wait(barrier, len(peers) + early.astype(jnp.int32) + G * last.astype(jnp.int32))
+
+    def prior_copy(i, src, dst, to):
+        return pltpu.make_async_remote_copy(
+            src_ref=src, dst_ref=dst, send_sem=s_prior.at[i], recv_sem=r_prior.at[i],
+            device_id=to, device_id_type=MESH)
+
+    up, down = s > 0, s < S - 1
+    to_down = prior_copy(0, ext.at[pl.ds(R * C, H * C)], ext.at[pl.ds(0, H * C)], (t, lax.rem(s + 1, S)))
+    to_up = prior_copy(1, ext.at[pl.ds(H * C, H * C)], ext.at[pl.ds((R + H) * C, H * C)], (t, lax.rem(s + S - 1, S)))
+    act_copy = prior_copy(2, actions, actn, (prv, s))
+    main = prior_copy(3, sendb, tnext, (prv, s))
+    act_copy.start()
+
+    @pl.when(down)
+    def _():
+        to_down.start()
+
+    @pl.when(up)
+    def _():
+        to_up.start()
+
+    main.start()
+    act_copy.wait_recv()
+    act = column(jnp.sum(column(actn[...]) * proj[...], axis=0, keepdims=True))
     biases = [column(hb[pl.ds(l, 1), :]) for l in range(layers)]
     biases[0] = biases[0] + act[:C]
     cb = column(cand_b[...])
@@ -133,12 +143,8 @@
             @pl.when(jnp.logical_not(down))
             def _():
                 ext[pl.ds((R + H) * C, H * C), :] = jnp.zeros((H * C, W), jnp.bfloat16)
-        elif H <= r < R + H and (r - H) % PR == 0:
-            main[(r - H) // PR].wait_recv()
         x = ext[pl.ds(r * C, C), :].astype(jnp.float32)
         put(ha, r, x)
-        if H <= r < R + H:
-            guess[pl.ds((r - H) * C, C), :] = jnp.where(t == 0, start_r[pl.ds((r - H) * C, C), :], x)
 
     src, dst = ha, hbuf
     wide = (Q + 2) * 3 * C
@@ -179,6 +185,12 @@
             src_ref=ab.at[j], dst_ref=rab.at[m], send_sem=s_ab.at[p], recv_sem=r_ab.at[p],
             device_id=(base + j, s), device_id_type=MESH)
 
+    def f0_copy(j):
+        return pltpu.make_async_remote_copy(
+            src_ref=f0.at[j], dst_ref=cin, send_sem=s_f0.at[j], recv_sem=r_f0.at[0],
+            device_id=(j, s), device_id_type=MESH)
+
+    main.wait_recv()
     acc = jnp.zeros((C, W), jnp.float32)
     for p in range(1, G + 1):
         j = lax.rem(m + p, G)
@@ -195,10 +207,15 @@
                     gate = jax.nn.sigmoid(hd[C:] + gb)
                     f = gate * x + (1.0 - gate) * cand
                     jac = gate + (1.0 - gate) * (1.0 - cand * cand) * skip
-                    d = traj[pl.ds(row, C, stride=R), :] - f
+                    d = tnext[pl.ds(pl.multiple_of(row * C, C), C), :].astype(jnp.float32) - f
                     acc = acc + d * d
                     ab[j, 0, pl.ds(own * C, C), :] = jac
                     ab[j, 1, pl.ds(own * C, C), :] = f - jac * x
+                    f0[j, own // per, pl.ds((own % per) * C, C), :] = f
+        @pl.when(last)
+        def _():
+            f0_copy(j).start()
+
         if p < G:
             ab_copy(p, j).start()
     rab[m] = ab[m]
@@ -206,10 +223,10 @@
 
     def ps_copy(p):
         return pltpu.make_async_remote_copy(
-            src_ref=part, dst_ref=rpart.at[p - 1], send_sem=s_ps.at[p - 1], recv_sem=r_ps.at[p - 1],
-            device_id=(t, lax.rem(s + p, S)), device_id_type=MESH)
-
-    for p in range(1, S):
+            src_ref=part, dst_ref=rpart.at[p], send_sem=s_ps.at[p], recv_sem=r_ps.at[p],
+            device_id=(nxt, lax.rem(s + p, S)), device_id_type=MESH)
+
+    for p in range(S):
         ps_copy(p).start()
     for p in range(1, G):
         ab_copy(p, lax.rem(m + p, G)).wait_recv()
@@ -225,11 +242,11 @@
             src_ref=ys.at[j, k], dst_ref=st.at[m, k], send_sem=s_st.at[p, k], recv_sem=r_st.at[p, k],
             device_id=(base + j, s), device_id_type=MESH)
 
+    @pl.when(early)
+    def _():
+        f0_copy(t).wait_recv()
+
     for k in range(K):
-        @pl.when(g == 0)
-        def _():
-            cin[k] = start_r[pl.ds(m * L + k * CH, CH), :]
-
         @pl.when(g > 0)
         def _():
             chain(k).wait_recv()
@@ -255,10 +272,10 @@
             for p in range(1, G):
                 st_copy(p, k).start()
 
-    total = part[...]
-    for p in range(1, S):
+    total = jnp.zeros((8, W), jnp.float32)
+    for p in range(S):
         ps_copy(p).wait_recv()
-        total = total + rpart[p - 1]
+        total = total + rpart[p]
     res[0] = jnp.sum(total) * (1.0 / (C * R * S * W))
 
     for k in range(K):
@@ -271,11 +288,15 @@
                 y = ys[m, k]
             for i in range(CH // C):
                 own = k * (CH // C) + i
-                out[pl.ds(j * RG + own, C, stride=R), :] = (
-                    ab[j, 0, pl.ds(own * C, C), :] * y[i * C:(i + 1) * C] + ab[j, 1, pl.ds(own * C, C), :])
-
-    for copy in main:
-        copy.wait_send()
+                out[pl.ds(j * RG + own, C, stride=R), :] = y[i * C:(i + 1) * C]
+
+    main.wait_send()
+    act_copy.wait_send()
+
+    @pl.when(last)
+    def _():
+        for j in range(G):
+            f0_copy(j).wait_send()
 
     @pl.when(down)
     def _():
@@ -285,7 +306,7 @@
     def _():
         to_up.wait_send()
 
-    for p in range(1, S):
+    for p in range(S):
         ps_copy(p).wait_send()
     for p in range(1, G):
         ab_copy(p, lax.rem(m + p, G)).wait_send()
@@ -320,7 +341,7 @@
     spec = pl.BlockSpec(memory_space=VMEM)
     new, res = pl.pallas_call(
         functools.partial(kernel, T, S, G, K, C, R, W, layers),
-        out_shape=(jax.ShapeDtypeStruct((C * R, W), f32), jax.ShapeDtypeStruct((1,), f32)),
+        out_shape=(VMEM((C * R, W), f32), jax.ShapeDtypeStruct((1,), f32)),
         in_specs=[pl.BlockSpec(memory_space=pltpu.HBM)] * 2 + [spec] * 8,
         out_specs=(spec, pl.BlockSpec(memory_space=pltpu.SMEM)),
         scratch_shapes=[
@@ -328,11 +349,13 @@
             VMEM((C * R, W), f32),
             VMEM((R * C, W), bf16),
             VMEM(((R + 2 * H) * C, W), bf16),
+            VMEM((R * C, W), bf16),
+            VMEM(actions.shape, f32),
+            VMEM((G, K, CH, W), f32),
             VMEM(((R + 2 * H) * 3 * C, W), bf16),
             VMEM(((R + 2 * H) * 3 * C, W), bf16),
             VMEM((layers, Q * C, wide), bf16),
             VMEM((Q * 2 * C, wide), bf16),
-            VMEM((R * C, W), f32),
             VMEM((R * C, W), f32),
             VMEM((G, 2, L, W), f32),
             VMEM((G, 2, L, W), f32),
@@ -341,13 +364,14 @@
             VMEM((G, K, CH, W), f32),
             VMEM((G, K, CH, W), f32),
             VMEM((8, W), f32),
-            VMEM((max(S - 1, 1), 8, W), f32),
+            VMEM((S, 8, W), f32),
             DMA((2,)),
-            DMA((2 + PARTS,)), DMA((2 + PARTS,)),
+            DMA((4,)), DMA((4,)),
             DMA((G,)), DMA((G,)),
             DMA((K,)), DMA((K,)),
             DMA((G, K)), DMA((G, K)),
-            DMA((max(S - 1, 1),)), DMA((max(S - 1, 1),)),
+            DMA((S,)), DMA((S,)),
+            DMA((G,)), DMA((1,)),
         ],
         compiler_params=pltpu.CompilerParams(
             collective_id=0, has_side_effects=True, vmem_limit_bytes=63 * 1024 * 1024),

time: 36.6 us -> 36.6 us (level)
  Pallas kernels: 32.3 us -> 33.3 us
  local copies, waits for them, and re-layouts: 1.67 us -> 0.71 us
    pallas_call x1, Pallas kernels: 32.3 us -> 33.3 us  [body(): pl.pallas_call(functools.partial(kernel, T, S, G, K, C, R, W, layers), ou...]
    unnamed x1, local copies, waits for them, and re-layouts: 1.67 us -> 0.71 us
where the time goes in v2:
time: 36.6 us; the launch traced here: 36.4 us
  Pallas kernels  33.3 us (91%)
  between operations  2.33 us (6%)
  local copies, waits for them, and re-layouts  0.71 us (2%)
    pallas_call x1, Pallas kernels, body(): pl.pallas_call(functools.partial(kernel, T, S, G, K, C, R, W, layers), ou...  33.3 us

profile of v2, /device:TPU:24, one launch (start us, length us, event | category | flops | bytes accessed | tf_op | source)
XLA Modules:
  0.0 36.4 jit_solution(3877712846858151587)
XLA Ops:
  0.6 33.3 %shard_map.113 = (f32[512,128]{1,0:T(8,128)S(1)}, f32[1]{0:T(128)}) custom-call(f32[512,128]{1,0:T(8,128)} %bitcast.11, f32[512,128]{1,0:T(8,128)} %bitcast.12, f32[1,16]{1,0:T(1,128)} %actions.1, bf16[864,32]{1,0:T(8,128)(2,1)} %bitcast.13, f32[3,32]{1,0:T(4,128)} %hb.1, bf16[288,64]{1,0:T(8,128)(2,1)} %bitcast.14, f32[1,32]{1,0:T(1,128)} %bitcast.15, ...), custom_call_target="tpu_custom_call" | custom-call | tf_op jit(solution)/shard_map/pallas_call | solution.py:342
  34.0 0.7 %copy.14 = f32[1,32,16,128]{3,2,1,0:T(8,128)} copy(f32[1,32,16,128]{3,2,1,0:T(8,128)S(1)} %bitcast.10) | data formatting | bytes 524288

commit v3 on v2

--- a/solution.py
+++ b/solution.py
@@ -217,7 +217,9 @@
             f0_copy(j).start()
 
         if p < G:
-            ab_copy(p, j).start()
+            @pl.when(jnp.logical_not(last))
+            def _():
+                ab_copy(p, j).start()
     rab[m] = ab[m]
     part[...] = jnp.sum(acc.reshape(C // 8, 8, W), axis=0)
 
@@ -229,7 +231,10 @@
     for p in range(S):
         ps_copy(p).start()
     for p in range(1, G):
-        ab_copy(p, lax.rem(m + p, G)).wait_recv()
+        @pl.when(base + lax.rem(m + G - p, G) != T - 1)
+        def _():
+            ab_copy(p, lax.rem(m + p, G)).wait_recv()
+
 
     def chain(k):
         return pltpu.make_async_remote_copy(
@@ -309,7 +314,10 @@
     for p in range(S):
         ps_copy(p).wait_send()
     for p in range(1, G):
-        ab_copy(p, lax.rem(m + p, G)).wait_send()
+        @pl.when(jnp.logical_not(last))
+        def _():
+            ab_copy(p, lax.rem(m + p, G)).wait_send()
+
         for k in range(K):
             st_copy(p, k).wait_send()
 

time: 36.6 us -> 36.6 us (level)
  no operation moved by 1% of the time
where the time goes in v3:
time: 36.6 us; the launch traced here: 36.4 us
  Pallas kernels  33.3 us (91%)
  between operations  2.33 us (6%)
  local copies, waits for them, and re-layouts  0.71 us (2%)
    pallas_call x1, Pallas kernels, body(): pl.pallas_call(functools.partial(kernel, T, S, G, K, C, R, W, layers), ou...  33.3 us

profile of v3, /device:TPU:24, one launch (start us, length us, event | category | flops | bytes accessed | tf_op | source)
XLA Modules:
  0.0 36.4 jit_solution(13971126996775302434)
XLA Ops:
  0.6 33.3 %shard_map.113 = (f32[512,128]{1,0:T(8,128)S(1)}, f32[1]{0:T(128)}) custom-call(f32[512,128]{1,0:T(8,128)} %bitcast.11, f32[512,128]{1,0:T(8,128)} %bitcast.12, f32[1,16]{1,0:T(1,128)} %actions.1, bf16[864,32]{1,0:T(8,128)(2,1)} %bitcast.13, f32[3,32]{1,0:T(4,128)} %hb.1, bf16[288,64]{1,0:T(8,128)(2,1)} %bitcast.14, f32[1,32]{1,0:T(1,128)} %bitcast.15, ...), custom_call_target="tpu_custom_call" | custom-call | tf_op jit(solution)/shard_map/pallas_call | solution.py:350
  34.0 0.7 %copy.14 = f32[1,32,16,128]{3,2,1,0:T(8,128)} copy(f32[1,32,16,128]{3,2,1,0:T(8,128)S(1)} %bitcast.10) | data formatting | bytes 524288

commit v4 on v1

--- a/solution.py
+++ b/solution.py
@@ -320,7 +320,7 @@
     spec = pl.BlockSpec(memory_space=VMEM)
     new, res = pl.pallas_call(
         functools.partial(kernel, T, S, G, K, C, R, W, layers),
-        out_shape=(jax.ShapeDtypeStruct((C * R, W), f32), jax.ShapeDtypeStruct((1,), f32)),
+        out_shape=(VMEM((C * R, W), f32), jax.ShapeDtypeStruct((1,), f32)),
         in_specs=[pl.BlockSpec(memory_space=pltpu.HBM)] * 2 + [spec] * 8,
         out_specs=(spec, pl.BlockSpec(memory_space=pltpu.SMEM)),
         scratch_shapes=[

time: 36.6 us -> 35.3 us (0.964)
  local copies, waits for them, and re-layouts: 1.67 us -> 0.71 us
    unnamed x1, local copies, waits for them, and re-layouts: 1.67 us -> 0.71 us
where the time goes in v4:
time: 35.3 us; the launch traced here: 35.2 us
  Pallas kernels  32.1 us (91%)
  between operations  2.33 us (7%)
  local copies, waits for them, and re-layouts  0.71 us (2%)
    pallas_call x1, Pallas kernels, body(): pl.pallas_call(functools.partial(kernel, T, S, G, K, C, R, W, layers), ou...  32.1 us

profile of v4, /device:TPU:24, one launch (start us, length us, event | category | flops | bytes accessed | tf_op | source)
XLA Modules:
  0.0 35.2 jit_solution(16092272546974741589)
XLA Ops:
  0.6 32.1 %shard_map.113 = (f32[512,128]{1,0:T(8,128)S(1)}, f32[1]{0:T(128)}) custom-call(f32[512,128]{1,0:T(8,128)} %bitcast.11, f32[512,128]{1,0:T(8,128)} %bitcast.12, f32[1,16]{1,0:T(1,128)} %actions.1, bf16[864,32]{1,0:T(8,128)(2,1)} %bitcast.13, f32[3,32]{1,0:T(4,128)} %hb.1, bf16[288,64]{1,0:T(8,128)(2,1)} %bitcast.14, f32[1,32]{1,0:T(1,128)} %bitcast.15, ...), custom_call_target="tpu_custom_call" | custom-call | tf_op jit(solution)/shard_map/pallas_call | solution.py:321
  32.8 0.7 %copy.14 = f32[1,32,16,128]{3,2,1,0:T(8,128)} copy(f32[1,32,16,128]{3,2,1,0:T(8,128)S(1)} %bitcast.10) | data formatting | bytes 524288
